TPU v7x, 512 devices: a whole 4x8x8 slice. The times are simulated.
512 devices in a mesh: heads: 8 (over z_lo, core), tm: 64 (over x, y, z_hi).
Axes of the slice: x: 4, y: 8, z: 8 (z_hi: 2, z_lo: 4; z = z_hi * 4 + z_lo), core: 2. Of those that a mesh axis runs over, the one named last changes fastest.
Arguments:
- queries: bfloat16 [16384, 3072], P('tm', 'heads'), parts along dimension 1, may hold values from -8 to 8
- keys: bfloat16 [16384, 3072], P('tm', 'heads'), parts along dimension 1, may hold values from -8 to 8
- values: bfloat16 [16384, 3072], P('tm', 'heads'), parts along dimension 1, may hold values from -6 to 6
- positions: int32 [3, 16384], P(None, 'tm'), may hold values from 0 to 79, as said below
- tile_masks: int32 [128, 8, 2], P('tm'), may hold values from 0 to 1, as said below
- sink_index: int32 [256], replicated, may hold values from 0 to 3599, as said below
Outputs:
- attended: bfloat16 [16384, 3072], P('tm', 'heads'), parts along dimension 1
There are 8 independent parts, one for each index of `heads`. A program takes and returns all parts, laid end to end along the dimension named above; an argument that names none is the same for every part. Nothing has to cross between parts.
Inputs may be any that keep to these rules, and one draw needn't show every extreme that they name: `positions`: consecutive tokens of the latent video of 33 x 45 x 80, row by row, from some starting token. `tile_masks`: tiles of farther partners are kept less often. `sink_index`: distinct rows among the first min(16384, 3600) of the window.
All inputs are finite; a program needn't handle non-finite values.
Results may differ from a plain program's by a relative error of at most 0.0085.
The roundings to bfloat16 on the way count: a program that leaves them out, or rounds other values in their place, can miss the bound.
Values may be sent and summed in bfloat16 or wider, within the bound.
A program may use at most 64 MiB of HBM per device.

v0:
```python
import jax
import jax.numpy as jnp
from jax import lax
from jax.sharding import PartitionSpec as P

HG = 3
HD = 128
TILE = 128
NOFF = 4
SINK = 256


def shifted(shard, axis, by):
    length = lax.axis_size(axis)
    pairs = [(i, i + by) for i in range(length) if 0 <= i + by < length]
    return lax.ppermute(shard, axis, pairs)


def rotate(row_data, position, factor):
    row_count = row_data.shape[0]
    first_size = HD // 8
    second_size = (HD - HD // 8) // 2
    section_sizes = (first_size, second_size, HD - first_size - second_size)
    angle_list = []
    for axis_id in range(3):
        section_width = section_sizes[axis_id]
        inverse = 256.0 ** (-jnp.arange(0, section_width, 2).astype(jnp.float32) / section_width)
        angle_list.append(position[axis_id].astype(jnp.float32)[:, None] * inverse[None, :])
    angle_all = jnp.concatenate(angle_list, axis=1)
    cosine = jnp.cos(angle_all)[:, None, :]
    sine_part = jnp.sin(angle_all)[:, None, :]
    pair_view = row_data.astype(jnp.float32).reshape(row_count, HG, HD // 2, 2)
    even_part = pair_view[..., 0]
    odd_part = pair_view[..., 1]
    turned = jnp.stack(
        [even_part * cosine - odd_part * sine_part, even_part * sine_part + odd_part * cosine],
        axis=-1,
    )
    return (turned * factor).reshape(row_count, HG * HD)


def block_part(query_heads, key_heads, value_heads, tile_keep):
    keep_mask = jnp.repeat(jnp.repeat(tile_keep, TILE, axis=0), TILE, axis=1)[:, None, :]
    scores = jnp.einsum("qhd,khd->qhk", query_heads, key_heads, preferred_element_type=jnp.float32)
    masked = jnp.where(keep_mask > 0, scores, -1e30)
    row_max = jnp.max(masked, axis=2)
    weights = jnp.exp(masked - row_max[:, :, None]) * keep_mask
    totals = jnp.sum(weights, axis=2)
    weighted = jnp.einsum(
        "qhk,khd->qhd",
        weights.astype(jnp.bfloat16),
        value_heads,
        preferred_element_type=jnp.float32,
    )
    return (weighted, row_max, totals)


def combine_parts(first, second):
    weighted_a, max_a, total_a = first
    weighted_b, max_b, total_b = second
    new_max = jnp.maximum(max_a, max_b)
    scale_first = jnp.exp(max_a - new_max)
    scale_second = jnp.exp(max_b - new_max)
    weighted = weighted_a * scale_first[:, :, None] + weighted_b * scale_second[:, :, None]
    return (weighted, new_max, total_a * scale_first + total_b * scale_second)


def on_device(queries, keys, values, positions, tile_masks, sink_index):
    rows_here = queries.shape[0]
    shards = lax.axis_size("tm")
    index_here = lax.axis_index("tm")
    feature_width = HG * HD
    tiles = rows_here // TILE
    q_rot = rotate(queries, positions, HD ** (-0.5)).astype(jnp.bfloat16)
    k_rot = rotate(keys, positions, 1.0).astype(jnp.bfloat16)
    query_heads = q_rot.reshape(rows_here, HG, HD)
    key_heads = k_rot.reshape(rows_here, HG, HD)
    value_heads = values.reshape(rows_here, HG, HD)
    state = block_part(query_heads, key_heads, value_heads, jnp.ones((tiles, tiles), jnp.float32))
    local_index = sink_index - index_here * rows_here
    one_hot = (local_index[:, None] == jnp.arange(rows_here, dtype=jnp.int32)[None, :]).astype(
        jnp.bfloat16
    )
    sink_table = jnp.dot(
        one_hot, jnp.concatenate([k_rot, values], axis=1), preferred_element_type=jnp.float32
    )
    sink_table = lax.psum(sink_table, "tm").astype(jnp.bfloat16)
    sink_keys = sink_table[:, :feature_width].reshape(SINK, HG, HD)
    sink_values = sink_table[:, feature_width:].reshape(SINK, HG, HD)
    sink_keep = jnp.ones((tiles, SINK // TILE), jnp.float32)
    state = combine_parts(state, block_part(query_heads, sink_keys, sink_values, sink_keep))
    mask_float = tile_masks.astype(jnp.float32)
    for offset in range(1, NOFF + 1):
        reverse_mask = tile_masks[:, NOFF + offset - 1, :].astype(jnp.bfloat16)
        their_queries, their_keys, their_values, their_mask = shifted(
            (q_rot, k_rot, values, reverse_mask), "tm", -offset
        )
        later_ok = (index_here + offset < shards).astype(jnp.float32)
        earlier_ok = (index_here - offset >= 0).astype(jnp.float32)
        mine_part = block_part(
            query_heads,
            their_keys.reshape(rows_here, HG, HD),
            their_values.reshape(rows_here, HG, HD),
            mask_float[:, offset - 1, :] * later_ok,
        )
        state = combine_parts(state, mine_part)
        returned = block_part(
            their_queries.reshape(rows_here, HG, HD),
            key_heads,
            value_heads,
            their_mask.astype(jnp.float32),
        )
        back_weighted, back_max, back_totals = shifted(
            (returned[0], returned[1], returned[2]), "tm", offset
        )
        back_max = jnp.where(earlier_ok > 0, back_max, -1e30)
        state = combine_parts(
            state, (back_weighted * earlier_ok, back_max, back_totals * earlier_ok)
        )
    weighted, row_max, totals = state
    return (weighted / totals[:, :, None]).astype(jnp.bfloat16).reshape(rows_here, feature_width)


def solution(mesh):
    in_specs = (
        P("tm", "heads"),
        P("tm", "heads"),
        P("tm", "heads"),
        P(None, "tm"),
        P("tm", None, None),
        P(),
    )
    out_specs = P("tm", "heads")
    return jax.shard_map(
        on_device, mesh=mesh, in_specs=in_specs, out_specs=out_specs, check_vma=False
    )
```

profile of v0, /device:TPU:4, one launch (start us, length us, event | category | flops | bytes accessed | tf_op | source)
XLA Modules:
  0.0 699.2 jit_solution(151011124536786140)
XLA Ops:
  0.0 13.8 %collective-permute-start.1 = (bf16[256,384]{1,0:T(8,128)(2,1)}, bf16[256,384]{1,0:T(8,128)(2,1)}, u32[]{:S(2)}, u32[]{:S(2)}) collective-permute-start(bf16[256,384]{1,0:T(8,128)(2,1)} %param.8), channel_id=1, source_target_pairs={{1,0},{2,1},{3,2},{4,3},{5,4},{6,5},{7,6},{8,7},{9,8},{10,9},{11,1... | collective-permute-start | bytes 589832 | tf_op jit(solution)/shard_map/ppermute | solution.py:16
  13.8 3.3 collective-permute-start.7
  17.1 4.0 collective-permute-start.19
  21.1 1.9 collective-permute-start.13
  23.0 0.8 fusion.95
  24.0 2.2 collective-permute-start.20
  26.3 1.1 copy.50
  28.6 0.4 fusion.63
  29.2 0.8 copy-done.12
  30.5 0.5 multiply_subtract_fusion.1
  31.0 0.5 maximum_convert_fusion
  32.6 0.6 copy-done.14
  33.5 404.2 %all-reduce.1 = bf16[256,768]{1,0:T(8,128)(2,1)S(1)} all-reduce(f32[256,768]{1,0:T(8,128)S(1)} %fusion.64), channel_id=1, replica_groups=mesh['heads'=8,'tm'=64] {'tm'}, use_global_device_ids=true, to_apply=%region_1.2 | all-reduce | flops 196608 | bytes 1179648 | tf_op jit(solution)/shard_map/psum | solution.py:87
  437.8 0.8 copy.56
  439.7 0.7 copy-done.1
  440.4 1.9 collective-permute-start.14
  442.4 8.1 %collective-permute-done.14 = bf16[2,2]{1,0:T(2,128)(2,1)S(1)} collective-permute-done((bf16[2,2]{1,0:T(2,128)(2,1)S(1)}, bf16[2,2]{1,0:T(2,128)(2,1)S(1)}, u32[]{:S(2)}, u32[]{:S(2)}) %collective-permute-start.14) | collective-permute-done | bytes 40 | tf_op jit(solution)/shard_map/ppermute | solution.py:16
  450.6 7.0 %collective-permute-start.8 = (bf16[2,2]{1,0:T(2,128)(2,1)S(1)}, bf16[2,2]{1,0:T(2,128)(2,1)S(1)}, u32[]{:S(2)}, u32[]{:S(2)}) collective-permute-start(bf16[2,2]{1,0:T(2,128)(2,1)S(1)} %get-tuple-element.7), channel_id=1, source_target_pairs={{2,0},{3,1},{4,2},{5,3},{6,4},{7,5},{8,6},{9,7},{10,8},{11,9},{12,... | collective-permute-start | bytes 32 | tf_op jit(solution)/shard_map/ppermute | solution.py:16
  457.8 1.1 collective-permute-done.8
  458.9 3.9 collective-permute-start.2
  463.0 5.3 collective-permute-done.2
  468.2 6.7 collective-permute-start.15
  475.2 6.5 collective-permute-done.15
  481.6 11.3 %collective-permute-start = (bf16[256,384]{0,1:T(8,128)(2,1)S(1)}, bf16[256,384]{0,1:T(8,128)(2,1)S(1)}, u32[]{:S(2)}, u32[]{:S(2)}) collective-permute-start(bf16[256,384]{0,1:T(8,128)(2,1)S(1)} %convert_element_type.180), channel_id=1, source_target_pairs={{1,0},{2,1},{3,2},{4,3},{5,4},{6,5},{7,6},{8,7},{9,8},{10,9},{11,1... | collective-permute-start | bytes 589832 | tf_op jit(solution)/shard_map/ppermute | solution.py:16
  493.2 1.0 convolution_bitcast_fusion.12
  494.3 1.8 collective-permute-done
  496.1 11.2 %collective-permute-start.6 = (bf16[256,384]{0,1:T(8,128)(2,1)S(1)}, bf16[256,384]{0,1:T(8,128)(2,1)S(1)}, u32[]{:S(2)}, u32[]{:S(2)}) collective-permute-start(bf16[256,384]{0,1:T(8,128)(2,1)S(1)} %convert_element_type.180), channel_id=1, source_target_pairs={{2,0},{3,1},{4,2},{5,3},{6,4},{7,5},{8,6},{9,7},{10,8},{11,9},{12,... | collective-permute-start | bytes 589832 | tf_op jit(solution)/shard_map/ppermute | solution.py:16
  507.6 2.8 collective-permute-done.6
  510.4 4.0 collective-permute-start.12
  514.7 8.0 %collective-permute-done.12 = bf16[256,384]{0,1:T(8,128)(2,1)S(1)} collective-permute-done((bf16[256,384]{0,1:T(8,128)(2,1)S(1)}, bf16[256,384]{0,1:T(8,128)(2,1)S(1)}, u32[]{:S(2)}, u32[]{:S(2)}) %collective-permute-start.12) | collective-permute-done | bytes 196640 | tf_op jit(solution)/shard_map/ppermute | solution.py:16
  522.8 3.9 collective-permute-start.18
  527.0 7.3 %collective-permute-done.18 = bf16[256,384]{0,1:T(8,128)(2,1)S(1)} collective-permute-done((bf16[256,384]{0,1:T(8,128)(2,1)S(1)}, bf16[256,384]{0,1:T(8,128)(2,1)S(1)}, u32[]{:S(2)}, u32[]{:S(2)}) %collective-permute-start.18) | collective-permute-done | bytes 196640 | tf_op jit(solution)/shard_map/ppermute | solution.py:16
  534.3 3.0 collective-permute-start.21
  537.6 5.2 collective-permute-done.21
  542.8 9.7 %collective-permute-start.9 = (bf16[256,384]{0,1:T(8,128)(2,1)S(1)}, bf16[256,384]{0,1:T(8,128)(2,1)S(1)}, u32[]{:S(2)}, u32[]{:S(2)}) collective-permute-start(bf16[256,384]{0,1:T(8,128)(2,1)S(1)} %convert_element_type.189), channel_id=1, source_target_pairs={{2,0},{3,1},{4,2},{5,3},{6,4},{7,5},{8,6},{9,7},{10,8},{11,9},{12,... | collective-permute-start | bytes 589832 | tf_op jit(solution)/shard_map/ppermute | solution.py:16
  552.9 4.9 collective-permute-done.9
  557.8 7.4 %collective-permute-start.3 = (bf16[256,384]{0,1:T(8,128)(2,1)S(1)}, bf16[256,384]{0,1:T(8,128)(2,1)S(1)}, u32[]{:S(2)}, u32[]{:S(2)}) collective-permute-start(bf16[256,384]{0,1:T(8,128)(2,1)S(1)} %convert_element_type.189), channel_id=1, source_target_pairs={{1,0},{2,1},{3,2},{4,3},{5,4},{6,5},{7,6},{8,7},{9,8},{10,9},{11,1... | collective-permute-start | bytes 589832 | tf_op jit(solution)/shard_map/ppermute | solution.py:16
  565.8 3.6 collective-permute-done.3
  569.3 15.0 %collective-permute-start.16 = (f32[256,3]{0,1:T(4,128)S(1)}, f32[256,3]{0,1:T(4,128)S(1)}, u32[]{:S(2)}, u32[]{:S(2)}) collective-permute-start(f32[256,3]{0,1:T(4,128)S(1)} %get-tuple-element.55), channel_id=1, source_target_pairs={{0,3},{1,4},{2,5},{3,6},{4,7},{5,8},{6,9},{7,10},{8,11},{9,12},{10... | collective-permute-start | bytes 9224 | tf_op jit(solution)/shard_map/ppermute | solution.py:16
  584.7 1.0 convolution_bitcast_fusion.10
  585.7 1.0 convolution_bitcast_fusion.14
  586.7 1.0 convolution_bitcast_fusion.16
  589.2 9.7 %collective-permute-start.10 = (f32[256,3]{0,1:T(4,128)S(1)}, f32[256,3]{0,1:T(4,128)S(1)}, u32[]{:S(2)}, u32[]{:S(2)}) collective-permute-start(f32[256,3]{0,1:T(4,128)S(1)} %get-tuple-element.59), channel_id=1, source_target_pairs={{0,2},{1,3},{2,4},{3,5},{4,6},{5,7},{6,8},{7,9},{8,10},{9,11},{10,... | collective-permute-start | bytes 9224 | tf_op jit(solution)/shard_map/ppermute | solution.py:16
  598.9 1.9 collective-permute-start.4
  601.0 1.7 copy.61
  602.7 1.7 copy.72
  604.5 9.0 %collective-permute-start.22 = (f32[256,3]{0,1:T(4,128)S(1)}, f32[256,3]{0,1:T(4,128)S(1)}, u32[]{:S(2)}, u32[]{:S(2)}) collective-permute-start(f32[256,3]{0,1:T(4,128)S(1)} %get-tuple-element.53), channel_id=1, source_target_pairs={{0,4},{1,5},{2,6},{3,7},{4,8},{5,9},{6,10},{7,11},{8,12},{9,13},{1... | collective-permute-start | bytes 9224 | tf_op jit(solution)/shard_map/ppermute | solution.py:16
  613.4 1.7 copy.94
  615.2 15.9 %collective-permute-start.27 = (f32[256,3]{0,1:T(4,128)S(1)}, f32[256,3]{0,1:T(4,128)S(1)}, u32[]{:S(2)}, u32[]{:S(2)}) collective-permute-start(f32[256,3]{0,1:T(4,128)S(1)} %fusion.51), channel_id=1, source_target_pairs={{0,4},{1,5},{2,6},{3,7},{4,8},{5,9},{6,10},{7,11},{8,12},{9,13},{1... | collective-permute-start | bytes 9224 | tf_op jit(solution)/shard_map/ppermute | solution.py:16
  631.1 1.7 copy.83
  632.9 8.1 %collective-permute-start.26 = (f32[256,3]{0,1:T(4,128)S(1)}, f32[256,3]{0,1:T(4,128)S(1)}, u32[]{:S(2)}, u32[]{:S(2)}) collective-permute-start(f32[256,3]{0,1:T(4,128)S(1)} %fusion.47), channel_id=1, source_target_pairs={{0,3},{1,4},{2,5},{3,6},{4,7},{5,8},{6,9},{7,10},{8,11},{9,12},{10... | collective-permute-start | bytes 9224 | tf_op jit(solution)/shard_map/ppermute | solution.py:16
  641.0 3.5 collective-permute-start.25
  644.5 7.3 %collective-permute-start.24 = (f32[256,3]{0,1:T(4,128)S(1)}, f32[256,3]{0,1:T(4,128)S(1)}, u32[]{:S(2)}, u32[]{:S(2)}) collective-permute-start(f32[256,3]{0,1:T(4,128)S(1)} %fusion.39), channel_id=1, source_target_pairs={{0,1},{1,2},{2,3},{3,4},{4,5},{5,6},{6,7},{7,8},{8,9},{9,10},{10,1... | collective-permute-start | bytes 9224 | tf_op jit(solution)/shard_map/ppermute | solution.py:16
  651.8 11.9 %collective-permute-start.23 = (f32[256,3,128]{0,2,1:T(8,128)}, f32[256,3,128]{0,2,1:T(8,128)S(1)}, u32[]{:S(2)}, u32[]{:S(2)}) collective-permute-start(f32[256,3,128]{0,2,1:T(8,128)} %convolution_bitcast_fusion.10), channel_id=1, source_target_pairs={{0,4},{1,5},{2,6},{3,7},{4,8},{5,9},{6,10},{7,11},{8,12},{9,13},{1... | collective-permute-start | bytes 1179656 | tf_op jit(solution)/shard_map/ppermute | solution.py:16
  663.8 1.9 collective-permute-start.17
  665.7 2.5 collective-permute-start.11
  668.2 7.3 %collective-permute-start.5 = (f32[256,3,128]{0,2,1:T(8,128)}, f32[256,3,128]{0,2,1:T(8,128)S(1)}, u32[]{:S(2)}, u32[]{:S(2)}) collective-permute-start(f32[256,3,128]{0,2,1:T(8,128)} %convolution_bitcast_fusion.16), channel_id=1, source_target_pairs={{0,1},{1,2},{2,3},{3,4},{4,5},{5,6},{6,7},{7,8},{8,9},{9,10},{10,1... | collective-permute-start | bytes 1179656 | tf_op jit(solution)/shard_map/ppermute | solution.py:16
  675.6 1.5 fusion.13
  677.4 0.6 copy-done.7
  678.3 0.8 copy-done.2
  679.8 7.0 %collective-permute-done.17 = f32[256,3,128]{0,2,1:T(8,128)S(1)} collective-permute-done((f32[256,3,128]{0,2,1:T(8,128)}, f32[256,3,128]{0,2,1:T(8,128)S(1)}, u32[]{:S(2)}, u32[]{:S(2)}) %collective-permute-start.17) | collective-permute-done | bytes 393248 | tf_op jit(solution)/shard_map/ppermute | solution.py:16
  686.8 11.1 %collective-permute-done.5 = f32[256,3,128]{0,2,1:T(8,128)S(1)} collective-permute-done((f32[256,3,128]{0,2,1:T(8,128)}, f32[256,3,128]{0,2,1:T(8,128)S(1)}, u32[]{:S(2)}, u32[]{:S(2)}) %collective-permute-start.5) | collective-permute-done | bytes 393248 | tf_op jit(solution)/shard_map/ppermute | solution.py:16
  697.9 0.5 fusion.32
  698.4 0.8 copy.102
  (124 shorter events, 10.7 us)
Async XLA Ops:
  0.0 589.1 %collective-permute-start.1 = (bf16[256,384]{1,0:T(8,128)(2,1)}, bf16[256,384]{1,0:T(8,128)(2,1)}, u32[]{:S(2)}, u32[]{:S(2)}) collective-permute-start(bf16[256,384]{1,0:T(8,128)(2,1)} %param.8), channel_id=1, source_target_pairs={{1,0},{2,1},{3,2},{4,3},{5,4},{6,5},{7,6},{8,7},{9,8},{10,9},{11,1... | collective-permute-start | bytes 589832 | tf_op jit(solution)/shard_map/ppermute | solution.py:16
  13.8 585.1 %collective-permute-start.7 = (bf16[256,384]{1,0:T(8,128)(2,1)}, bf16[256,384]{1,0:T(8,128)(2,1)}, u32[]{:S(2)}, u32[]{:S(2)}) collective-permute-start(bf16[256,384]{1,0:T(8,128)(2,1)} %param.8), channel_id=1, source_target_pairs={{2,0},{3,1},{4,2},{5,3},{6,4},{7,5},{8,6},{9,7},{10,8},{11,9},{12,... | collective-permute-start | bytes 589832 | tf_op jit(solution)/shard_map/ppermute | solution.py:16
  17.1 587.4 %collective-permute-start.19 = (bf16[256,384]{1,0:T(8,128)(2,1)}, bf16[256,384]{1,0:T(8,128)(2,1)}, u32[]{:S(2)}, u32[]{:S(2)}) collective-permute-start(bf16[256,384]{1,0:T(8,128)(2,1)} %param.8), channel_id=1, source_target_pairs={{4,0},{5,1},{6,2},{7,3},{8,4},{9,5},{10,6},{11,7},{12,8},{13,9},{1... | collective-permute-start | bytes 589832 | tf_op jit(solution)/shard_map/ppermute | solution.py:16
  21.1 594.1 %collective-permute-start.13 = (bf16[256,384]{1,0:T(8,128)(2,1)}, bf16[256,384]{1,0:T(8,128)(2,1)}, u32[]{:S(2)}, u32[]{:S(2)}) collective-permute-start(bf16[256,384]{1,0:T(8,128)(2,1)} %param.8), channel_id=1, source_target_pairs={{3,0},{4,1},{5,2},{6,3},{7,4},{8,5},{9,6},{10,7},{11,8},{12,9},{13... | collective-permute-start | bytes 589832 | tf_op jit(solution)/shard_map/ppermute | solution.py:16
  24.0 416.4 %collective-permute-start.20 = (bf16[2,2]{1,0:T(2,128)(2,1)S(1)}, bf16[2,2]{1,0:T(2,128)(2,1)S(1)}, u32[]{:S(2)}, u32[]{:S(2)}) collective-permute-start(bf16[2,2]{1,0:T(2,128)(2,1)S(1)} %get-tuple-element.5), channel_id=1, source_target_pairs={{4,0},{5,1},{6,2},{7,3},{8,4},{9,5},{10,6},{11,7},{12,8},{13,9},{1... | collective-permute-start | bytes 32 | tf_op jit(solution)/shard_map/ppermute | solution.py:16
  26.3 1.1 copy-start.13
  26.3 1.1 copy-start.11
  29.1 0.9 copy-start.12
  32.5 0.7 copy-start.14
  439.4 0.9 copy-start.1
  440.4 10.2 %collective-permute-start.14 = (bf16[2,2]{1,0:T(2,128)(2,1)S(1)}, bf16[2,2]{1,0:T(2,128)(2,1)S(1)}, u32[]{:S(2)}, u32[]{:S(2)}) collective-permute-start(bf16[2,2]{1,0:T(2,128)(2,1)S(1)} %get-tuple-element.6), channel_id=1, source_target_pairs={{3,0},{4,1},{5,2},{6,3},{7,4},{8,5},{9,6},{10,7},{11,8},{12,9},{13... | collective-permute-start | bytes 32 | tf_op jit(solution)/shard_map/ppermute | solution.py:16
  450.6 8.3 %collective-permute-start.8 = (bf16[2,2]{1,0:T(2,128)(2,1)S(1)}, bf16[2,2]{1,0:T(2,128)(2,1)S(1)}, u32[]{:S(2)}, u32[]{:S(2)}) collective-permute-start(bf16[2,2]{1,0:T(2,128)(2,1)S(1)} %get-tuple-element.7), channel_id=1, source_target_pairs={{2,0},{3,1},{4,2},{5,3},{6,4},{7,5},{8,6},{9,7},{10,8},{11,9},{12,... | collective-permute-start | bytes 32 | tf_op jit(solution)/shard_map/ppermute | solution.py:16
  458.9 9.3 %collective-permute-start.2 = (bf16[2,2]{1,0:T(2,128)(2,1)S(1)}, bf16[2,2]{1,0:T(2,128)(2,1)S(1)}, u32[]{:S(2)}, u32[]{:S(2)}) collective-permute-start(bf16[2,2]{1,0:T(2,128)(2,1)S(1)} %get-tuple-element.8), channel_id=1, source_target_pairs={{1,0},{2,1},{3,2},{4,3},{5,4},{6,5},{7,6},{8,7},{9,8},{10,9},{11,1... | collective-permute-start | bytes 32 | tf_op jit(solution)/shard_map/ppermute | solution.py:16
  468.2 13.4 %collective-permute-start.15 = (bf16[256,384]{0,1:T(8,128)(2,1)S(1)}, bf16[256,384]{0,1:T(8,128)(2,1)S(1)}, u32[]{:S(2)}, u32[]{:S(2)}) collective-permute-start(bf16[256,384]{0,1:T(8,128)(2,1)S(1)} %convert_element_type.189), channel_id=1, source_target_pairs={{3,0},{4,1},{5,2},{6,3},{7,4},{8,5},{9,6},{10,7},{11,8},{12,9},{13... | collective-permute-start | bytes 589832 | tf_op jit(solution)/shard_map/ppermute | solution.py:16
  481.6 14.4 %collective-permute-start = (bf16[256,384]{0,1:T(8,128)(2,1)S(1)}, bf16[256,384]{0,1:T(8,128)(2,1)S(1)}, u32[]{:S(2)}, u32[]{:S(2)}) collective-permute-start(bf16[256,384]{0,1:T(8,128)(2,1)S(1)} %convert_element_type.180), channel_id=1, source_target_pairs={{1,0},{2,1},{3,2},{4,3},{5,4},{6,5},{7,6},{8,7},{9,8},{10,9},{11,1... | collective-permute-start | bytes 589832 | tf_op jit(solution)/shard_map/ppermute | solution.py:16
  496.1 14.3 %collective-permute-start.6 = (bf16[256,384]{0,1:T(8,128)(2,1)S(1)}, bf16[256,384]{0,1:T(8,128)(2,1)S(1)}, u32[]{:S(2)}, u32[]{:S(2)}) collective-permute-start(bf16[256,384]{0,1:T(8,128)(2,1)S(1)} %convert_element_type.180), channel_id=1, source_target_pairs={{2,0},{3,1},{4,2},{5,3},{6,4},{7,5},{8,6},{9,7},{10,8},{11,9},{12,... | collective-permute-start | bytes 589832 | tf_op jit(solution)/shard_map/ppermute | solution.py:16
  507.6 80.3 %copy-start.3 = (f32[256,3,256]{0,2,1:T(8,128)}, f32[256,3,256]{0,2,1:T(8,128)S(1)}, u32[]{:S(2)}) copy-start(f32[256,3,256]{0,2,1:T(8,128)S(1)} %get-tuple-element.66) | copy-start | bytes 2359300
  510.4 12.4 %collective-permute-start.12 = (bf16[256,384]{0,1:T(8,128)(2,1)S(1)}, bf16[256,384]{0,1:T(8,128)(2,1)S(1)}, u32[]{:S(2)}, u32[]{:S(2)}) collective-permute-start(bf16[256,384]{0,1:T(8,128)(2,1)S(1)} %convert_element_type.180), channel_id=1, source_target_pairs={{3,0},{4,1},{5,2},{6,3},{7,4},{8,5},{9,6},{10,7},{11,8},{12,9},{13... | collective-permute-start | bytes 589832 | tf_op jit(solution)/shard_map/ppermute | solution.py:16
  522.8 11.5 %collective-permute-start.18 = (bf16[256,384]{0,1:T(8,128)(2,1)S(1)}, bf16[256,384]{0,1:T(8,128)(2,1)S(1)}, u32[]{:S(2)}, u32[]{:S(2)}) collective-permute-start(bf16[256,384]{0,1:T(8,128)(2,1)S(1)} %convert_element_type.180), channel_id=1, source_target_pairs={{4,0},{5,1},{6,2},{7,3},{8,4},{9,5},{10,6},{11,7},{12,8},{13,9},{1... | collective-permute-start | bytes 589832 | tf_op jit(solution)/shard_map/ppermute | solution.py:16
  534.3 8.5 %collective-permute-start.21 = (bf16[256,384]{0,1:T(8,128)(2,1)S(1)}, bf16[256,384]{0,1:T(8,128)(2,1)S(1)}, u32[]{:S(2)}, u32[]{:S(2)}) collective-permute-start(bf16[256,384]{0,1:T(8,128)(2,1)S(1)} %convert_element_type.189), channel_id=1, source_target_pairs={{4,0},{5,1},{6,2},{7,3},{8,4},{9,5},{10,6},{11,7},{12,8},{13,9},{1... | collective-permute-start | bytes 589832 | tf_op jit(solution)/shard_map/ppermute | solution.py:16
  537.6 50.6 %copy-start = (f32[256,3,256]{0,2,1:T(8,128)}, f32[256,3,256]{0,2,1:T(8,128)S(1)}, u32[]{:S(2)}) copy-start(f32[256,3,256]{0,2,1:T(8,128)S(1)} %get-tuple-element.52) | copy-start | bytes 2359300
  542.8 15.0 %collective-permute-start.9 = (bf16[256,384]{0,1:T(8,128)(2,1)S(1)}, bf16[256,384]{0,1:T(8,128)(2,1)S(1)}, u32[]{:S(2)}, u32[]{:S(2)}) collective-permute-start(bf16[256,384]{0,1:T(8,128)(2,1)S(1)} %convert_element_type.189), channel_id=1, source_target_pairs={{2,0},{3,1},{4,2},{5,3},{6,4},{7,5},{8,6},{9,7},{10,8},{11,9},{12,... | collective-permute-start | bytes 589832 | tf_op jit(solution)/shard_map/ppermute | solution.py:16
  557.8 11.5 %collective-permute-start.3 = (bf16[256,384]{0,1:T(8,128)(2,1)S(1)}, bf16[256,384]{0,1:T(8,128)(2,1)S(1)}, u32[]{:S(2)}, u32[]{:S(2)}) collective-permute-start(bf16[256,384]{0,1:T(8,128)(2,1)S(1)} %convert_element_type.189), channel_id=1, source_target_pairs={{1,0},{2,1},{3,2},{4,3},{5,4},{6,5},{7,6},{8,7},{9,8},{10,9},{11,1... | collective-permute-start | bytes 589832 | tf_op jit(solution)/shard_map/ppermute | solution.py:16
  569.3 63.5 %collective-permute-start.16 = (f32[256,3]{0,1:T(4,128)S(1)}, f32[256,3]{0,1:T(4,128)S(1)}, u32[]{:S(2)}, u32[]{:S(2)}) collective-permute-start(f32[256,3]{0,1:T(4,128)S(1)} %get-tuple-element.55), channel_id=1, source_target_pairs={{0,3},{1,4},{2,5},{3,6},{4,7},{5,8},{6,9},{7,10},{8,11},{9,12},{10... | collective-permute-start | bytes 9224 | tf_op jit(solution)/shard_map/ppermute | solution.py:16
  588.1 0.7 copy-start.5
  589.2 51.8 %collective-permute-start.10 = (f32[256,3]{0,1:T(4,128)S(1)}, f32[256,3]{0,1:T(4,128)S(1)}, u32[]{:S(2)}, u32[]{:S(2)}) collective-permute-start(f32[256,3]{0,1:T(4,128)S(1)} %get-tuple-element.59), channel_id=1, source_target_pairs={{0,2},{1,3},{2,4},{3,5},{4,6},{5,7},{6,8},{7,9},{8,10},{9,11},{10,... | collective-permute-start | bytes 9224 | tf_op jit(solution)/shard_map/ppermute | solution.py:16
  598.9 45.6 %collective-permute-start.4 = (f32[256,3]{0,1:T(4,128)S(1)}, f32[256,3]{0,1:T(4,128)S(1)}, u32[]{:S(2)}, u32[]{:S(2)}) collective-permute-start(f32[256,3]{0,1:T(4,128)S(1)} %get-tuple-element.63), channel_id=1, source_target_pairs={{0,1},{1,2},{2,3},{3,4},{4,5},{5,6},{6,7},{7,8},{8,9},{9,10},{10,1... | collective-permute-start | bytes 9224 | tf_op jit(solution)/shard_map/ppermute | solution.py:16
  604.5 59.3 %collective-permute-start.22 = (f32[256,3]{0,1:T(4,128)S(1)}, f32[256,3]{0,1:T(4,128)S(1)}, u32[]{:S(2)}, u32[]{:S(2)}) collective-permute-start(f32[256,3]{0,1:T(4,128)S(1)} %get-tuple-element.53), channel_id=1, source_target_pairs={{0,4},{1,5},{2,6},{3,7},{4,8},{5,9},{6,10},{7,11},{8,12},{9,13},{1... | collective-permute-start | bytes 9224 | tf_op jit(solution)/shard_map/ppermute | solution.py:16
  615.2 36.7 %collective-permute-start.27 = (f32[256,3]{0,1:T(4,128)S(1)}, f32[256,3]{0,1:T(4,128)S(1)}, u32[]{:S(2)}, u32[]{:S(2)}) collective-permute-start(f32[256,3]{0,1:T(4,128)S(1)} %fusion.51), channel_id=1, source_target_pairs={{0,4},{1,5},{2,6},{3,7},{4,8},{5,9},{6,10},{7,11},{8,12},{9,13},{1... | collective-permute-start | bytes 9224 | tf_op jit(solution)/shard_map/ppermute | solution.py:16
  632.8 42.7 %copy-start.8 = (bf16[256,384]{0,1:T(8,128)(2,1)S(1)}, bf16[256,384]{0,1:T(8,128)(2,1)}, u32[]{:S(2)}) copy-start(bf16[256,384]{0,1:T(8,128)(2,1)} %copy.94) | copy-start | bytes 589828
  632.9 32.9 %collective-permute-start.26 = (f32[256,3]{0,1:T(4,128)S(1)}, f32[256,3]{0,1:T(4,128)S(1)}, u32[]{:S(2)}, u32[]{:S(2)}) collective-permute-start(f32[256,3]{0,1:T(4,128)S(1)} %fusion.47), channel_id=1, source_target_pairs={{0,3},{1,4},{2,5},{3,6},{4,7},{5,8},{6,9},{7,10},{8,11},{9,12},{10... | collective-permute-start | bytes 9224 | tf_op jit(solution)/shard_map/ppermute | solution.py:16
  641.0 27.2 %collective-permute-start.25 = (f32[256,3]{0,1:T(4,128)S(1)}, f32[256,3]{0,1:T(4,128)S(1)}, u32[]{:S(2)}, u32[]{:S(2)}) collective-permute-start(f32[256,3]{0,1:T(4,128)S(1)} %fusion.43), channel_id=1, source_target_pairs={{0,2},{1,3},{2,4},{3,5},{4,6},{5,7},{6,8},{7,9},{8,10},{9,11},{10,... | collective-permute-start | bytes 9224 | tf_op jit(solution)/shard_map/ppermute | solution.py:16
  644.5 31.0 %collective-permute-start.24 = (f32[256,3]{0,1:T(4,128)S(1)}, f32[256,3]{0,1:T(4,128)S(1)}, u32[]{:S(2)}, u32[]{:S(2)}) collective-permute-start(f32[256,3]{0,1:T(4,128)S(1)} %fusion.39), channel_id=1, source_target_pairs={{0,1},{1,2},{2,3},{3,4},{4,5},{5,6},{6,7},{7,8},{8,9},{9,10},{10,1... | collective-permute-start | bytes 9224 | tf_op jit(solution)/shard_map/ppermute | solution.py:16
  651.8 27.9 %collective-permute-start.23 = (f32[256,3,128]{0,2,1:T(8,128)}, f32[256,3,128]{0,2,1:T(8,128)S(1)}, u32[]{:S(2)}, u32[]{:S(2)}) collective-permute-start(f32[256,3,128]{0,2,1:T(8,128)} %convolution_bitcast_fusion.10), channel_id=1, source_target_pairs={{0,4},{1,5},{2,6},{3,7},{4,8},{5,9},{6,10},{7,11},{8,12},{9,13},{1... | collective-permute-start | bytes 1179656 | tf_op jit(solution)/shard_map/ppermute | solution.py:16
  663.8 23.0 %collective-permute-start.17 = (f32[256,3,128]{0,2,1:T(8,128)}, f32[256,3,128]{0,2,1:T(8,128)S(1)}, u32[]{:S(2)}, u32[]{:S(2)}) collective-permute-start(f32[256,3,128]{0,2,1:T(8,128)} %convolution_bitcast_fusion.12), channel_id=1, source_target_pairs={{0,3},{1,4},{2,5},{3,6},{4,7},{5,8},{6,9},{7,10},{8,11},{9,12},{10... | collective-permute-start | bytes 1179656 | tf_op jit(solution)/shard_map/ppermute | solution.py:16
  665.7 21.1 %collective-permute-start.11 = (f32[256,3,128]{0,2,1:T(8,128)}, f32[256,3,128]{0,2,1:T(8,128)S(1)}, u32[]{:S(2)}, u32[]{:S(2)}) collective-permute-start(f32[256,3,128]{0,2,1:T(8,128)} %convolution_bitcast_fusion.14), channel_id=1, source_target_pairs={{0,2},{1,3},{2,4},{3,5},{4,6},{5,7},{6,8},{7,9},{8,10},{9,11},{10,... | collective-permute-start | bytes 1179656 | tf_op jit(solution)/shard_map/ppermute | solution.py:16
  668.2 29.7 %collective-permute-start.5 = (f32[256,3,128]{0,2,1:T(8,128)}, f32[256,3,128]{0,2,1:T(8,128)S(1)}, u32[]{:S(2)}, u32[]{:S(2)}) collective-permute-start(f32[256,3,128]{0,2,1:T(8,128)} %convolution_bitcast_fusion.16), channel_id=1, source_target_pairs={{0,1},{1,2},{2,3},{3,4},{4,5},{5,6},{6,7},{7,8},{8,9},{9,10},{10,1... | collective-permute-start | bytes 1179656 | tf_op jit(solution)/shard_map/ppermute | solution.py:16
  675.6 1.5 copy-start.9
  677.1 0.9 copy-start.7
  678.0 1.1 copy-start.2
  678.0 1.2 copy-start.10
  679.5 18.4 %copy-start.4 = (f32[256,3,256]{0,2,1:T(8,128)S(1)}, f32[256,3,256]{0,2,1:T(8,128)}, u32[]{:S(2)}) copy-start(f32[256,3,256]{0,2,1:T(8,128)} %copy-done.3) | copy-start | bytes 2359300
  679.5 18.4 %copy-start.6 = (bf16[256,384]{0,1:T(8,128)(2,1)S(1)}, bf16[256,384]{0,1:T(8,128)(2,1)}, u32[]{:S(2)}) copy-start(bf16[256,384]{0,1:T(8,128)(2,1)} %copy.61) | copy-start | bytes 589828
where the time goes:
time: 700 us; the launch traced here: 699 us
  blocking collectives  404 us (58%)
  starting transfers between devices  189 us (27%)
  waiting for transfers between devices  72.8 us (10%)
  local copies, waits for them, and re-layouts  16.8 us (2%)
  matrix products  10.8 us (2%)
    psum x1, blocking collectives, on_device(): sink_table = lax.psum(sink_table, 'tm').astype(jnp.bfloat16)  404 us
    ppermute x28, starting transfers between devices, shifted(): return lax.ppermute(shard, axis, pairs)  189 us
    ppermute x28, waiting for transfers between devices, shifted(): return lax.ppermute(shard, axis, pairs)  72.8 us
  transfers between devices with their start and end apart: 28, of which 13 were waited for; matrix products, arithmetic and copies ran while one was open for 4% of the time, Pallas kernels for 0%

commit v1 on v0

v1 whole, which is shorter than its diff:
```python
import functools

import jax
import jax.numpy as jnp
from jax import lax
from jax.experimental import pallas as pl
from jax.experimental.pallas import tpu as pltpu
from jax.sharding import PartitionSpec as P

MESH = pl.DeviceIdType.MESH
HG = 3
HD = 128
ROWS = 256
TILE = 128
SINK = 256
NX, NY = 4, 8
NP = NX * NY
CH = 16
MASKED = -1e30
FLOOR = -1e28
BF = jnp.bfloat16
F32 = jnp.float32
NT = (((1,), (1,)), ((), ()))


def iota(shape, dim):
    return lax.broadcasted_iota(jnp.int32, shape, dim)


def kernel(
    q_ref, k_ref, v_ref, pos_ref, sink_ref, mask_ref, out_ref,
    kv, qb, bias_own, bias_send, bias_recv, acc, ml, o_send, o_recv, ml_recv,
    ptab, tab, scat, sink_bias,
    s_kv, r_kv, s_q, r_q, s_b, r_b, s_sc, r_sc, s_y, r_y, s_x, r_x, s_o, r_o, s_ml, r_ml,
):
    head = lax.axis_index("heads")
    me = lax.axis_index("tm")
    z = me % 2
    p = me // 2
    x = p // NY
    y = p % NY
    kvi = x % 2
    half = x // 2

    def dev(pp, zz):
        return (head, pp * 2 + zz)

    def remote(src, dst, ssem, rsem, target):
        return pltpu.make_async_remote_copy(
            src_ref=src, dst_ref=dst, send_sem=ssem, recv_sem=rsem,
            device_id=target, device_id_type=MESH,
        )

    partner = dev(p, 1 - z)
    after = dev((p + 1) % NP, z)
    before = dev((p + NP - 1) % NP, z)

    barrier = pltpu.get_barrier_semaphore()
    pl.semaphore_signal(barrier, inc=1, device_id=partner, device_id_type=MESH)

    def greet(i, carry):
        pl.semaphore_signal(barrier, inc=1, device_id=dev((p + i) % NP, z), device_id_type=MESH)
        return carry

    lax.fori_loop(1, NP, greet, 0)

    d_of = iota((HD, ROWS), 0)
    first = d_of < 16
    second = d_of < 72
    posf = pos_ref[...].astype(F32)
    coord = jnp.where(first, posf[0:1], jnp.where(second, posf[1:2], posf[2:3]))
    pair = jnp.where(first, d_of, jnp.where(second, d_of - 16, d_of - 72)) // 2
    width = jnp.where(first, 16.0, 56.0).astype(F32)
    inverse = jnp.exp2(pair.astype(F32) * (-16.0) / width)
    angle = (coord * inverse).T
    lane = iota((ROWS, HD), 1)
    cosine = jnp.cos(angle)
    sine = jnp.sin(angle)
    sine = jnp.where(lane % 2 == 0, -sine, sine)
    r_id = iota((HD, HD), 0)
    c_id = iota((HD, HD), 1)
    swap = (r_id + 1 - 2 * (r_id % 2) == c_id).astype(BF)
    eye = (r_id == c_id).astype(BF)

    def rotated(ref, h, factor):
        part = ref[:, h * HD:(h + 1) * HD]
        other = jnp.dot(part, swap, preferred_element_type=F32)
        return ((part.astype(F32) * cosine + other * sine) * factor).astype(BF)

    for h in range(HG):
        kv[2, h, 0:ROWS, :] = rotated(k_ref, h, 1.0)
        turned = lax.dot_general(
            eye, v_ref[:, h * HD:(h + 1) * HD], NT, preferred_element_type=F32
        ).astype(BF)
        kv[2, h, ROWS:ROWS + HD, :] = turned[:, 0:TILE]
        kv[2, h, ROWS + HD:ROWS + 2 * HD, :] = turned[:, TILE:]
    for h in range(HG):
        qb[0, h] = rotated(q_ref, h, HD ** -0.5)

    sink_col = jnp.broadcast_to(sink_ref[...].astype(F32), (HD, SINK)).T.astype(jnp.int32)
    sink_bias[...] = jnp.where((sink_col // ROWS) % 2 == z, 0.0, MASKED).astype(F32)

    @pl.when(x == 0)
    def _():
        local = sink_col - me * ROWS
        hot = jnp.concatenate([local == lane, local == lane + HD], axis=1).astype(F32).astype(BF)
        for h in range(HG):
            cols = slice(h * HD, (h + 1) * HD)
            ptab[0, :, cols] = jnp.dot(
                hot, kv[2, h, 0:ROWS, :], preferred_element_type=F32
            ).astype(BF)
            ptab[1, :, cols] = jnp.dot(
                hot, v_ref[:, cols], preferred_element_type=F32
            ).astype(BF)

    wide = iota((1, ROWS), 1) < TILE

    def mask_row(offset, kt):
        slot = offset - 1 if offset > 0 else 4 - offset - 1
        other = me + offset
        inside = jnp.where((other >= 0) & (other < 2 * NP), 1, 0)
        both = [
            ((mask_ref[qt, slot, kt] * inside).astype(F32) - 1.0) * (-MASKED) for qt in range(2)
        ]
        return jnp.where(wide, both[0], both[1])

    for i, offset in enumerate((-4, -2, 2, 4)):
        for kt in range(2):
            bias_own[2 * i + kt:2 * i + kt + 1, :] = mask_row(offset, kt)
    for i, offset in enumerate((-3, -1, 1, 3)):
        for kt in range(2):
            bias_send[2 * i + kt:2 * i + kt + 1, :] = mask_row(offset, kt)

    pl.semaphore_wait(barrier, NP)

    def scatter(i):
        t = (p + i) % NP
        tx = t // NY
        row = pl.multiple_of((tx // 2) * (SINK // 2) + (t % NY) * CH, CH)
        return remote(
            ptab.at[tx % 2, pl.ds(row, CH)], scat.at[y], s_sc.at[i], r_sc.at[y], dev(t, z)
        )

    @pl.when(x == 0)
    def _():
        def go(i, carry):
            scatter(i).start()
            return carry

        lax.fori_loop(1, NP, go, 0)
        scat[y] = ptab[0, pl.ds(pl.multiple_of(y * CH, CH), CH), :]

    bias_copy = remote(bias_send, bias_recv, s_b, r_b, partner)
    bias_copy.start()
    q_copies = [remote(qb.at[0, h], qb.at[1, h], s_q.at[h], r_q.at[h], partner) for h in range(HG)]
    up = [remote(kv.at[2, h], kv.at[1, h], s_kv.at[0, h], r_kv.at[0, h], after) for h in range(HG)]
    down = [
        remote(kv.at[2, h], kv.at[3, h], s_kv.at[1, h], r_kv.at[1, h], before) for h in range(HG)
    ]
    up2 = [remote(kv.at[1, h], kv.at[0, h], s_kv.at[2, h], r_kv.at[2, h], after) for h in range(HG)]
    down2 = [
        remote(kv.at[3, h], kv.at[4, h], s_kv.at[3, h], r_kv.at[3, h], before) for h in range(HG)
    ]
    for h in range(HG):
        up[h].start()
        down[h].start()
        q_copies[h].start()

    for t in range(2):
        for h in range(HG):
            ml[t, h, 0:1, :] = jnp.full((1, ROWS), FLOOR, F32)
            ml[t, h, 1:2, :] = jnp.zeros((1, ROWS), F32)
            acc[t, h] = jnp.zeros((HD, ROWS), F32)

    def attend(t, h, blocks):
        query = qb[t, h]
        m_old = ml[t, h, 0:1, :]
        m_new = m_old
        scores = []
        for key, _, rows, key_bias in blocks:
            s = lax.dot_general(key(), query, NT, preferred_element_type=F32)
            if key_bias is not None:
                s = s + key_bias()
            for kt in range(2):
                part = jnp.max(s[kt * TILE:(kt + 1) * TILE], axis=0, keepdims=True)
                m_new = jnp.maximum(m_new, part if rows is None else part + rows[kt])
            scores.append(s)
        alpha = jnp.exp(m_old - m_new)
        total = ml[t, h, 1:2, :] * alpha
        result = acc[t, h] * alpha
        for (_, value, rows, _), s in zip(blocks, scores):
            weights = []
            for kt in range(2):
                level = m_new if rows is None else m_new - rows[kt]
                w = jnp.exp(s[kt * TILE:(kt + 1) * TILE] - level)
                total = total + jnp.sum(w, axis=0, keepdims=True)
                weights.append(w.astype(BF))
            result = result + jnp.dot(
                value(), jnp.concatenate(weights, axis=0), preferred_element_type=F32
            )
        acc[t, h] = result
        ml[t, h, 0:1, :] = m_new
        ml[t, h, 1:2, :] = total

    def shard_block(slot, h, rows):
        def key():
            return kv[slot, h, 0:ROWS, :]

        def value():
            return jnp.concatenate(
                [kv[slot, h, ROWS:ROWS + HD, :], kv[slot, h, ROWS + HD:ROWS + 2 * HD, :]], axis=1
            )

        return (key, value, rows, None)

    def own_rows(i):
        return [bias_own[2 * i + kt:2 * i + kt + 1, :] for kt in range(2)]

    def their_rows(even, odd):
        return [
            jnp.where(
                z == 0,
                bias_recv[2 * even + kt:2 * even + kt + 1, :],
                bias_recv[2 * odd + kt:2 * odd + kt + 1, :],
            )
            for kt in range(2)
        ]

    def sink_block(h):
        cols = slice(h * HD, (h + 1) * HD)

        def value():
            return lax.dot_general(eye, tab[1, :, cols], NT, preferred_element_type=F32).astype(BF)

        def key_bias():
            b = sink_bias[...]
            return jnp.concatenate([b, b], axis=1)

        return (lambda: tab[0, :, cols], value, None, key_bias)

    attend(0, 0, [shard_block(2, 0, None)])

    def arrived(i):
        return remote(
            ptab.at[0, pl.ds(0, CH)], scat.at[i], s_sc.at[0], r_sc.at[i], partner
        )

    def take(i, carry):
        @pl.when((x > 0) | (y != i))
        def _():
            arrived(i).wait_recv()

        return carry

    lax.fori_loop(0, NY, take, 0)
    chunk = scat[0].astype(F32)
    for i in range(1, NY):
        chunk = chunk + scat[i].astype(F32)
    base = half * (SINK // 2)

    def chunk_at(yy):
        return tab.at[kvi, pl.ds(pl.multiple_of(base + yy * CH, CH), CH)]

    tab[kvi, pl.ds(pl.multiple_of(base + y * CH, CH), CH), :] = chunk.astype(BF)

    def along_y(i):
        return remote(
            chunk_at(y), chunk_at(y), s_y.at[i], r_y.at[i], dev(x * NY + (y + i) % NY, z)
        )

    def from_y(i):
        there = chunk_at((y + NY - i) % NY)
        return remote(there, there, s_y.at[i], r_y.at[i], partner)

    def send_y(i, carry):
        along_y(i).start()
        return carry

    lax.fori_loop(1, NY, send_y, 0)

    for h in range(HG):
        up[h].wait_recv()
        up2[h].start()
        down[h].wait_recv()
        down2[h].start()
        if h == 0:
            attend(0, 1, [shard_block(2, 1, None)])
        if h == 1:
            attend(0, 2, [shard_block(2, 2, None)])

            def take_y(i, carry):
                from_y(i).wait_recv()
                return carry

            lax.fori_loop(1, NY, take_y, 0)

            def quarter(xx):
                row = pl.multiple_of((xx // 2) * (SINK // 2), SINK // 2)
                return tab.at[xx % 2, pl.ds(row, SINK // 2)]

            def along_x(i):
                return remote(
                    quarter(x), quarter(x), s_x.at[i], r_x.at[i], dev(((x + i) % NX) * NY + y, z)
                )

            def from_x(i):
                there = quarter((x + NX - i) % NX)
                return remote(there, there, s_x.at[i], r_x.at[i], partner)

            for i in range(1, NX):
                along_x(i).start()

    bias_copy.wait_recv()
    for h in range(HG):
        q_copies[h].wait_recv()
        attend(0, h, [shard_block(1, h, own_rows(1)), shard_block(3, h, own_rows(2))])
        attend(
            1,
            h,
            [
                shard_block(1, h, their_rows(0, 1)),
                shard_block(2, h, their_rows(1, 2)),
                shard_block(3, h, their_rows(2, 3)),
            ],
        )
    for i in range(1, NX):
        from_x(i).wait_recv()
    for h in range(HG):
        attend(1, h, [sink_block(h)])
        attend(0, h, [sink_block(h)])

    far = 4 * (1 - z)
    o_copies = []
    for h in range(HG):
        up2[h].wait_recv()
        down2[h].wait_recv()
        attend(1, h, [shard_block(far, h, their_rows(3, 0))])
        o_send[h] = acc[1, h].astype(BF)
        o_copies.append(remote(o_send.at[h], o_recv.at[h], s_o.at[h], r_o.at[h], partner))
        o_copies[-1].start()
        o_copies.append(remote(ml.at[1, h], ml_recv.at[h], s_ml.at[h], r_ml.at[h], partner))
        o_copies[-1].start()
        attend(0, h, [shard_block(0, h, own_rows(0)), shard_block(4, h, own_rows(3))])

    r_big = iota((ROWS, ROWS), 0)
    c_big = iota((ROWS, ROWS), 1)
    eye_big = (r_big == c_big).astype(BF)
    for h in range(HG):
        o_copies[2 * h].wait_recv()
        o_copies[2 * h + 1].wait_recv()
        m_a = ml[0, h, 0:1, :]
        m_b = ml_recv[h, 0:1, :]
        m_all = jnp.maximum(m_a, m_b)
        scale_a = jnp.exp(m_a - m_all)
        scale_b = jnp.exp(m_b - m_all)
        total = ml[0, h, 1:2, :] * scale_a + ml_recv[h, 1:2, :] * scale_b
        result = acc[0, h] * scale_a + o_recv[h].astype(F32) * scale_b
        result = (result / total).astype(BF)
        out_ref[:, h * HD:(h + 1) * HD] = lax.dot_general(
            eye_big, result, NT, preferred_element_type=F32
        ).astype(BF)

    @pl.when(x == 0)
    def _():
        def gone(i, carry):
            scatter(i).wait_send()
            return carry

        lax.fori_loop(1, NP, gone, 0)

    bias_copy.wait_send()
    for h in range(HG):
        for c in (q_copies, up, down, up2, down2):
            c[h].wait_send()

    def gone_y(i, carry):
        along_y(i).wait_send()
        return carry

    lax.fori_loop(1, NY, gone_y, 0)
    for i in range(1, NX):
        along_x(i).wait_send()
    for c in o_copies:
        c.wait_send()


def on_device(queries, keys, values, positions, tile_masks, sink_index):
    vmem = pl.BlockSpec(memory_space=pltpu.VMEM)
    smem = pl.BlockSpec(memory_space=pltpu.SMEM)
    dma = pltpu.SemaphoreType.DMA
    return pl.pallas_call(
        kernel,
        out_shape=jax.ShapeDtypeStruct(queries.shape, BF),
        in_specs=[vmem, vmem, vmem, vmem, vmem, smem],
        out_specs=vmem,
        scratch_shapes=[
            pltpu.VMEM((5, HG, 2 * ROWS, HD), BF),
            pltpu.VMEM((2, HG, ROWS, HD), BF),
            pltpu.VMEM((8, ROWS), F32),
            pltpu.VMEM((8, ROWS), F32),
            pltpu.VMEM((8, ROWS), F32),
            pltpu.VMEM((2, HG, HD, ROWS), F32),
            pltpu.VMEM((2, HG, 8, ROWS), F32),
            pltpu.VMEM((HG, HD, ROWS), BF),
            pltpu.VMEM((HG, HD, ROWS), BF),
            pltpu.VMEM((HG, 8, ROWS), F32),
            pltpu.VMEM((2, SINK, HG * HD), BF),
            pltpu.VMEM((2, SINK, HG * HD), BF),
            pltpu.VMEM((NY, CH, HG * HD), BF),
            pltpu.VMEM((SINK, HD), F32),
            dma((4, HG)), dma((4, HG)), dma((HG,)), dma((HG,)), dma, dma,
            dma((NP,)), dma((NY,)), dma((NY,)), dma((NY,)), dma((NX,)), dma((NX,)),
            dma((HG,)), dma((HG,)), dma((HG,)), dma((HG,)),
        ],
        compiler_params=pltpu.CompilerParams(
            collective_id=0, has_side_effects=True, vmem_limit_bytes=40 << 20
        ),
        cost_estimate=pl.CostEstimate(
            flops=2 * 11 * 2 * ROWS * ROWS * HD * HG, bytes_accessed=4 << 20,
            transcendentals=11 * ROWS * ROWS * HG,
        ),
    )(queries, keys, values, positions, sink_index[None, :], tile_masks)


def solution(mesh):
    in_specs = (
        P("tm", "heads"), P("tm", "heads"), P("tm", "heads"), P(None, "tm"), P("tm", None, None), P(),
    )
    return jax.shard_map(
        on_device, mesh=mesh, in_specs=in_specs, out_specs=P("tm", "heads"), check_vma=False
    )
```

time: 700 us -> 69 us (0.10)
  blocking collectives: 404 us -> 0 us
  starting transfers between devices: 189 us -> 0 us
  waiting for transfers between devices: 72.8 us -> 0 us
  Pallas kernels: 0 us -> 64.5 us
  local copies, waits for them, and re-layouts: 16.8 us -> 4.26 us
  matrix products: 10.8 us -> 0 us
    psum x1 -> x0, blocking collectives: 404 us -> none  [on_device(): sink_table = lax.psum(sink_table, 'tm').astype(jnp.bfloat16)]
    ppermute x28 -> x0, starting transfers between devices: 189 us -> none  [shifted(): return lax.ppermute(shard, axis, pairs)]
    ppermute x28 -> x0, waiting for transfers between devices: 72.8 us -> none  [shifted(): return lax.ppermute(shard, axis, pairs)]
    pallas_call x0 -> x1, Pallas kernels: none -> 64.5 us  [on_device(): pl.pallas_call(kernel, out_shape=jax.ShapeDtypeStruct(queries.shape, BF),...]
    dot_general x21 -> x0, matrix products: 10.8 us -> none  [the longest x10 7.19 us: block_part(): jnp.einsum('qhk,khd->qhd', weights.astype(jnp.bfloat16), value_heads, pre...]
  transfers between devices with their start and end apart: 28 -> 0, of which waited for: 13 -> 0; matrix products, arithmetic and copies ran while one was open for 4% -> 0% of each run, Pallas kernels for 0% -> 0%
where the time goes in v1:
time: 69 us; the launch traced here: 68.8 us
  Pallas kernels  64.5 us (93%)
  local copies, waits for them, and re-layouts  4.26 us (6%)
    pallas_call x1, Pallas kernels, on_device(): pl.pallas_call(kernel, out_shape=jax.ShapeDtypeStruct(queries.shape, BF),...  64.5 us
    unnamed x12, local copies, waits for them, and re-layouts  4.26 us

profile of v1, /device:TPU:4, one launch (start us, length us, event | category | flops | bytes accessed | tf_op | source)
XLA Modules:
  0.0 68.8 jit_solution(7479594291271822404)
XLA Ops:
  0.0 0.0 copy-start.3
  0.0 0.0 copy-start.4
  0.0 0.8 %copy.7.mask_ref = s32[2,8,2]{2,1,0:T(8,128)S(1)} copy(s32[2,8,2]{1,2,0:T(2,128)} %param.10) | data formatting | bytes 256 | tf_op args[4]
  0.8 0.0 copy-done.3
  0.8 0.0 copy-done.4
  0.8 0.0 copy-start
  0.8 0.9 %copy-done = bf16[256,384]{1,0:T(8,128)(2,1)S(1)} copy-done((bf16[256,384]{1,0:T(8,128)(2,1)S(1)}, bf16[256,384]{1,0:T(8,128)(2,1)}, u32[]{:S(2)}) %copy-start) | copy-done | bytes 196632
  1.7 0.0 copy-start.1
  1.7 0.9 %copy-done.1 = bf16[256,384]{1,0:T(8,128)(2,1)S(1)} copy-done((bf16[256,384]{1,0:T(8,128)(2,1)S(1)}, bf16[256,384]{1,0:T(8,128)(2,1)}, u32[]{:S(2)}) %copy-start.1) | copy-done | bytes 196632
  2.7 0.0 copy-start.2
  2.7 0.9 %copy-done.2 = bf16[256,384]{1,0:T(8,128)(2,1)S(1)} copy-done((bf16[256,384]{1,0:T(8,128)(2,1)S(1)}, bf16[256,384]{1,0:T(8,128)(2,1)}, u32[]{:S(2)}) %copy-start.2) | copy-done | bytes 196632
  3.6 64.5 %shard_map.64 = bf16[256,384]{1,0:T(8,128)(2,1)S(1)} custom-call(bf16[256,384]{1,0:T(8,128)(2,1)S(1)} %copy-done, bf16[256,384]{1,0:T(8,128)(2,1)S(1)} %copy-done.1, bf16[256,384]{1,0:T(8,128)(2,1)S(1)} %copy-done.2, s32[3,256]{1,0:T(4,128)S(1)} %copy-done.3, s32[1,256]{1,0:T(1,128)S(1)} %bitcast.1, s32[2,8,2]{2,1,0:T(8,128)S(1)} %copy.7.mask_ref), custom_call_target="tpu_custom_call" | custom-call | flops 1107296256 | bytes 4194304 | tf_op jit(solution)/shard_map/pallas_call | solution.py:391
  68.1 0.7 copy.9
Async XLA Ops:
  0.0 0.8 %copy-start.3 = (s32[3,256]{1,0:T(4,128)S(1)}, s32[3,256]{1,0:T(4,128)}, u32[]{:S(2)}) copy-start(s32[3,256]{1,0:T(4,128)} %pos_ref.1) | copy-start | bytes 9220
  0.0 0.8 %copy-start.4 = (s32[256]{0:T(256)S(1)}, s32[256]{0:T(256)}, u32[]{:S(2)}) copy-start(s32[256]{0:T(256)} %param.11) | copy-start | bytes 3076
  0.8 0.9 %copy-start = (bf16[256,384]{1,0:T(8,128)(2,1)S(1)}, bf16[256,384]{1,0:T(8,128)(2,1)}, u32[]{:S(2)}) copy-start(bf16[256,384]{1,0:T(8,128)(2,1)} %q_ref.1) | copy-start | bytes 589828
  1.7 0.9 %copy-start.1 = (bf16[256,384]{1,0:T(8,128)(2,1)S(1)}, bf16[256,384]{1,0:T(8,128)(2,1)}, u32[]{:S(2)}) copy-start(bf16[256,384]{1,0:T(8,128)(2,1)} %k_ref.1) | copy-start | bytes 589828
  2.7 0.9 %copy-start.2 = (bf16[256,384]{1,0:T(8,128)(2,1)S(1)}, bf16[256,384]{1,0:T(8,128)(2,1)}, u32[]{:S(2)}) copy-start(bf16[256,384]{1,0:T(8,128)(2,1)} %v_ref.1) | copy-start | bytes 589828

commit v2 on v1

v2 whole, which is shorter than its diff:
```python
import functools

import jax
import jax.numpy as jnp
from jax import lax
from jax.experimental import pallas as pl
from jax.experimental.pallas import tpu as pltpu
from jax.sharding import PartitionSpec as P

MESH = pl.DeviceIdType.MESH
HG = 3
HD = 128
ROWS = 256
TILE = 128
SINK = 256
NX, NY = 4, 8
NP = NX * NY
CH = 16
KEPT = (0, 2)
MASKED = -1e30
FLOOR = -1e28
BF = jnp.bfloat16
F32 = jnp.float32
NT = (((1,), (1,)), ((), ()))


def iota(shape, dim):
    return lax.broadcasted_iota(jnp.int32, shape, dim)


def kernel(
    q_hbm, k_hbm, v_hbm, pos_hbm, sink_hbm, mask_hbm, out_ref,
    q_ref, k_ref, v_ref, pos_ref, sink_ref, mask_ref,
    kv, qb, bias_own, bias_send, bias_recv, acc, ml, o_send, o_recv, ml_recv,
    ptab, tab, quart, scat, z_send, z_recv, c_send,
    s_in, s_kv, r_kv, s_q, r_q, s_b, r_b, s_sc, r_sc, s_a, r_a, s_z, r_z, s_c, r_c, s_y, r_y,
    s_x, r_x, s_o, r_o, s_ml, r_ml,
):
    head = lax.axis_index("heads")
    me = lax.axis_index("tm")
    z = me % 2
    p = me // 2
    x = p // NY
    y = p % NY
    kvi = x % 2
    half = x // 2

    def dev(pp, zz):
        return (head, pp * 2 + zz)

    def remote(src, dst, ssem, rsem, target):
        return pltpu.make_async_remote_copy(
            src_ref=src, dst_ref=dst, send_sem=ssem, recv_sem=rsem,
            device_id=target, device_id_type=MESH,
        )

    partner = dev(p, 1 - z)
    after = dev((p + 1) % NP, z)
    before = dev((p + NP - 1) % NP, z)

    def on_y(i):
        return dev(x * NY + (y + i) % NY, z)

    def on_x(i):
        return dev(((x + i) % NX) * NY + y, z)

    near = [partner, after, before]
    near += [on_x(i) for i in range(1, NX)] + [on_y(i) for i in range(1, NY)]
    barrier = pltpu.get_barrier_semaphore()
    for target in near:
        pl.semaphore_signal(barrier, inc=1, device_id=target, device_id_type=MESH)

    loads = [
        pltpu.make_async_copy(src, dst, s_in.at[i])
        for i, (src, dst) in enumerate(
            [(pos_hbm, pos_ref), (k_hbm, k_ref), (v_hbm, v_ref), (sink_hbm, sink_ref),
             (mask_hbm, mask_ref), (q_hbm, q_ref)]
        )
    ]
    for c in loads:
        c.start()
    loads[0].wait()

    d_of = iota((HD, ROWS), 0)
    first = d_of < 16
    second = d_of < 72
    posf = pos_ref[...].astype(F32)
    coord = jnp.where(first, posf[0:1], jnp.where(second, posf[1:2], posf[2:3]))
    pair = jnp.where(first, d_of, jnp.where(second, d_of - 16, d_of - 72)) // 2
    width = jnp.where(first, 16.0, 56.0).astype(F32)
    inverse = jnp.exp2(pair.astype(F32) * (-16.0) / width)
    angle = (coord * inverse).T
    lane = iota((ROWS, HD), 1)
    cosine = jnp.cos(angle)
    sine = jnp.sin(angle)
    sine = jnp.where(lane % 2 == 0, -sine, sine)
    r_id = iota((HD, HD), 0)
    c_id = iota((HD, HD), 1)
    swap = (r_id + 1 - 2 * (r_id % 2) == c_id).astype(BF)
    eye = (r_id == c_id).astype(BF)

    def rotated(ref, h, factor):
        part = ref[:, h * HD:(h + 1) * HD]
        other = jnp.dot(part, swap, preferred_element_type=F32)
        return ((part.astype(F32) * cosine + other * sine) * factor).astype(BF)

    loads[1].wait()
    loads[2].wait()
    for h in range(HG):
        kv[2, h, 0:ROWS, :] = rotated(k_ref, h, 1.0)
        turned = lax.dot_general(
            eye, v_ref[:, h * HD:(h + 1) * HD], NT, preferred_element_type=F32
        ).astype(BF)
        kv[2, h, ROWS:ROWS + HD, :] = turned[:, 0:TILE]
        kv[2, h, ROWS + HD:ROWS + 2 * HD, :] = turned[:, TILE:]

    loads[3].wait()

    spread_to = [i for i in range(1, NX) if i not in KEPT]
    gets_quarter = functools.reduce(lambda a, b: a | b, [x == i for i in spread_to], x < 0)
    gets_chunk = functools.reduce(lambda a, b: a | b, [x == i for i in KEPT[1:]], x < 0)

    def spread(i):
        return remote(
            ptab.at[i % 2, pl.ds((i // 2) * (SINK // 2), SINK // 2)], quart,
            s_sc.at[i], r_sc, on_x(i),
        )

    @pl.when(x == 0)
    def _():
        sink_col = jnp.broadcast_to(sink_ref[...].astype(F32), (HD, SINK)).T.astype(jnp.int32)
        local = sink_col - me * ROWS
        hot = jnp.concatenate([local == lane, local == lane + HD], axis=1).astype(F32).astype(BF)
        for h in range(HG):
            cols = slice(h * HD, (h + 1) * HD)
            ptab[0, :, cols] = jnp.dot(
                hot, kv[2, h, 0:ROWS, :], preferred_element_type=F32
            ).astype(BF)
            ptab[1, :, cols] = jnp.dot(
                hot, v_ref[:, cols], preferred_element_type=F32
            ).astype(BF)

    pl.semaphore_wait(barrier, len(near))

    up = [remote(kv.at[2, h], kv.at[1, h], s_kv.at[0, h], r_kv.at[0, h], after) for h in range(HG)]
    down = [
        remote(kv.at[2, h], kv.at[3, h], s_kv.at[1, h], r_kv.at[1, h], before) for h in range(HG)
    ]
    up2 = [remote(kv.at[1, h], kv.at[0, h], s_kv.at[2, h], r_kv.at[2, h], after) for h in range(HG)]
    down2 = [
        remote(kv.at[3, h], kv.at[4, h], s_kv.at[3, h], r_kv.at[3, h], before) for h in range(HG)
    ]

    @pl.when(x == 0)
    def _():
        for i in spread_to:
            spread(i).start()

    def send_kv(h):
        up[h].start()
        down[h].start()

    send_kv(0)


    loads[4].wait()
    loads[5].wait()
    for h in range(HG):
        qb[0, h] = rotated(q_ref, h, HD ** -0.5)
    wide = iota((1, ROWS), 1) < TILE

    def mask_row(offset, kt):
        slot = offset - 1 if offset > 0 else 4 - offset - 1
        other = me + offset
        inside = jnp.where((other >= 0) & (other < 2 * NP), 1, 0)
        both = [
            ((mask_ref[qt, kt, slot] * inside).astype(F32) - 1.0) * (-MASKED) for qt in range(2)
        ]
        return jnp.where(wide, both[0], both[1])

    for i, offset in enumerate((-3, -1, 1, 3)):
        for kt in range(2):
            bias_send[2 * i + kt:2 * i + kt + 1, :] = mask_row(offset, kt)
    bias_copy = remote(bias_send, bias_recv, s_b, r_b, partner)
    bias_copy.start()
    q_copies = [remote(qb.at[0, h], qb.at[1, h], s_q.at[h], r_q.at[h], partner) for h in range(HG)]
    for h in range(HG):
        q_copies[h].start()
    for i, offset in enumerate((-4, -2, 2, 4)):
        for kt in range(2):
            bias_own[2 * i + kt:2 * i + kt + 1, :] = mask_row(offset, kt)


    for t in range(2):
        for h in range(HG):
            ml[t, h, 0:1, :] = jnp.full((1, ROWS), FLOOR, F32)
            ml[t, h, 1:2, :] = jnp.zeros((1, ROWS), F32)
            acc[t, h] = jnp.zeros((HD, ROWS), F32)

    def attend(t, h, blocks):
        query = qb[t, h]
        m_old = ml[t, h, 0:1, :]
        m_new = m_old
        scores = []
        for key, _, rows in blocks:
            s = lax.dot_general(key(), query, NT, preferred_element_type=F32)
            for kt in range(2):
                part = jnp.max(s[kt * TILE:(kt + 1) * TILE], axis=0, keepdims=True)
                m_new = jnp.maximum(m_new, part if rows is None else part + rows[kt])
            scores.append(s)
        alpha = jnp.exp(m_old - m_new)
        total = ml[t, h, 1:2, :] * alpha
        result = acc[t, h] * alpha
        for (_, value, rows), s in zip(blocks, scores):
            weights = []
            for kt in range(2):
                level = m_new if rows is None else m_new - rows[kt]
                w = jnp.exp(s[kt * TILE:(kt + 1) * TILE] - level)
                total = total + jnp.sum(w, axis=0, keepdims=True)
                weights.append(w.astype(BF))
            result = result + jnp.dot(
                value(), jnp.concatenate(weights, axis=0), preferred_element_type=F32
            )
        acc[t, h] = result
        ml[t, h, 0:1, :] = m_new
        ml[t, h, 1:2, :] = total

    def shard_block(slot, h, rows):
        def key():
            return kv[slot, h, 0:ROWS, :]

        def value():
            return jnp.concatenate(
                [kv[slot, h, ROWS:ROWS + HD, :], kv[slot, h, ROWS + HD:ROWS + 2 * HD, :]], axis=1
            )

        return (key, value, rows)

    def own_rows(i):
        return [bias_own[2 * i + kt:2 * i + kt + 1, :] for kt in range(2)]

    def their_rows(even, odd):
        return [
            jnp.where(
                z == 0,
                bias_recv[2 * even + kt:2 * even + kt + 1, :],
                bias_recv[2 * odd + kt:2 * odd + kt + 1, :],
            )
            for kt in range(2)
        ]

    def sink_block(h):
        cols = slice(h * HD, (h + 1) * HD)

        def value():
            return lax.dot_general(eye, tab[1, :, cols], NT, preferred_element_type=F32).astype(BF)

        return (lambda: tab[0, :, cols], value, None)

    def hop(h):
        up[h].wait_recv()
        up2[h].start()
        down[h].wait_recv()
        down2[h].start()

    def near_blocks(h):
        q_copies[h].wait_recv()
        attend(
            1,
            h,
            [
                shard_block(1, h, their_rows(0, 1)),
                shard_block(2, h, their_rows(1, 2)),
                shard_block(3, h, their_rows(2, 3)),
            ],
        )
        attend(0, h, [shard_block(1, h, own_rows(1)), shard_block(3, h, own_rows(2))])

    far = 4 * (1 - z)
    o_copies = [remote(o_send.at[h], o_recv.at[h], s_o.at[h], r_o.at[h], partner) for h in range(HG)]
    ml_copies = [
        remote(ml.at[1, h], ml_recv.at[h], s_ml.at[h], r_ml.at[h], partner) for h in range(HG)
    ]

    def far_blocks(h):
        up2[h].wait_recv()
        down2[h].wait_recv()
        attend(1, h, [shard_block(far, h, their_rows(3, 0))])
        o_send[h] = acc[1, h].astype(BF)
        o_copies[h].start()
        ml_copies[h].start()
        attend(0, h, [shard_block(0, h, own_rows(0)), shard_block(4, h, own_rows(3))])

    base = half * (SINK // 2)

    def chunk_at(yy):
        return tab.at[kvi, pl.ds(pl.multiple_of(base + yy * CH, CH), CH)]

    def quarter(xx):
        row = pl.multiple_of((xx // 2) * (SINK // 2), SINK // 2)
        return tab.at[xx % 2, pl.ds(row, SINK // 2)]

    def part_of(yy):
        return pl.ds(pl.multiple_of(yy * CH, CH), CH)

    def row_of(u, yy):
        return pl.ds(pl.multiple_of((u // 2) * (SINK // 2) + yy * CH, CH), CH)

    kept_copies = [
        remote(
            ptab.at[u % 2, row_of(u, (y + i) % NY)], scat.at[j, i], s_a.at[j, i], r_a.at[j, i], on_y(i)
        )
        for j, u in enumerate(KEPT) for i in range(1, NY)
    ]
    a_copies = [
        remote(quart.at[part_of((y + i) % NY)], scat.at[0, i], s_a.at[0, i], r_a.at[0, i], on_y(i))
        for i in range(1, NY)
    ]
    kept_z = remote(z_send, z_recv, s_z, r_z, partner)
    z_copy = remote(z_send.at[0], z_recv.at[0], s_z, r_z, partner)
    c_copies = [
        remote(c_send.at[j], tab.at[u % 2, row_of(u, y)], s_c.at[j], r_c, on_x(u))
        for j, u in enumerate(KEPT) if j > 0
    ]
    c_arrival = remote(c_send.at[0], chunk_at(y), s_c.at[0], r_c, partner)
    y_copies = [
        remote(chunk_at(y), chunk_at(y), s_y.at[i], r_y.at[i], on_y(i)) for i in range(1, NY)
    ]
    y_arrivals = [
        remote(chunk_at((y + NY - i) % NY), chunk_at((y + NY - i) % NY), s_y.at[i], r_y.at[i], partner)
        for i in range(1, NY)
    ]
    x_copies = [
        remote(quarter(x), quarter(x), s_x.at[i], r_x.at[i], on_x(i)) for i in range(1, NX)
    ]
    x_arrivals = [
        remote(quarter((x + NX - i) % NX), quarter((x + NX - i) % NX), s_x.at[i], r_x.at[i], partner)
        for i in range(1, NX)
    ]

    def sink_exchange():
        @pl.when(x == 0)
        def _():
            for c in kept_copies:
                c.start()

        @pl.when(gets_quarter)
        def _():
            spread(1).wait_recv()
            for c in a_copies:
                c.start()

    def sink_sum():
        @pl.when(x == 0)
        def _():
            for c in kept_copies:
                c.wait_recv()
            for j, u in enumerate(KEPT):
                chunk = ptab[u % 2, row_of(u, y), :].astype(F32)
                for i in range(1, NY):
                    chunk = chunk + scat[j, i].astype(F32)
                z_send[j] = chunk.astype(BF)
            kept_z.start()

        @pl.when(gets_quarter)
        def _():
            for c in a_copies:
                c.wait_recv()
            chunk = quart[part_of(y), :].astype(F32)
            for i in range(1, NY):
                chunk = chunk + scat[0, i].astype(F32)
            z_send[0] = chunk.astype(BF)
            z_copy.start()

    def sink_finish():
        @pl.when(x == 0)
        def _():
            kept_z.wait_recv()
            for j in range(1, len(KEPT)):
                c_send[j] = (z_send[j].astype(F32) + z_recv[j].astype(F32)).astype(BF)
                c_copies[j - 1].start()

        @pl.when(gets_quarter)
        def _():
            z_copy.wait_recv()

        @pl.when(gets_chunk)
        def _():
            c_arrival.wait_recv()

        @pl.when((x == 0) | gets_quarter)
        def _():
            chunk = z_send[0].astype(F32) + z_recv[0].astype(F32)
            tab[kvi, pl.ds(pl.multiple_of(base + y * CH, CH), CH), :] = chunk.astype(BF)

        for c in y_copies:
            c.start()

    def sink_along_x():
        for c in y_arrivals:
            c.wait_recv()
        for c in x_copies:
            c.start()

    attend(0, 0, [shard_block(2, 0, None)])
    send_kv(1)
    attend(0, 1, [shard_block(2, 1, None)])
    attend(0, 2, [shard_block(2, 2, None)])
    sink_exchange()
    hop(0)
    send_kv(2)
    bias_copy.wait_recv()
    near_blocks(0)
    sink_sum()
    hop(1)
    near_blocks(1)
    sink_finish()
    hop(2)
    far_blocks(0)
    near_blocks(2)
    sink_along_x()
    far_blocks(1)
    far_blocks(2)
    for c in x_arrivals:
        c.wait_recv()
    for h in range(HG):
        attend(0, h, [sink_block(h)])

    r_big = iota((ROWS, ROWS), 0)
    c_big = iota((ROWS, ROWS), 1)
    eye_big = (r_big == c_big).astype(BF)
    for h in range(HG):
        o_copies[h].wait_recv()
        ml_copies[h].wait_recv()
        m_a = ml[0, h, 0:1, :]
        m_b = ml_recv[h, 0:1, :]
        m_all = jnp.maximum(m_a, m_b)
        scale_a = jnp.exp(m_a - m_all)
        scale_b = jnp.exp(m_b - m_all)
        total = ml[0, h, 1:2, :] * scale_a + ml_recv[h, 1:2, :] * scale_b
        result = acc[0, h] * scale_a + o_recv[h].astype(F32) * scale_b
        result = (result / total).astype(BF)
        out_ref[:, h * HD:(h + 1) * HD] = lax.dot_general(
            eye_big, result, NT, preferred_element_type=F32
        ).astype(BF)

    @pl.when(x == 0)
    def _():
        for i in spread_to:
            spread(i).wait_send()

    for group in (q_copies, up, down, up2, down2, o_copies, ml_copies, y_copies, x_copies):
        for c in group:
            c.wait_send()
    bias_copy.wait_send()

    @pl.when(x == 0)
    def _():
        kept_z.wait_send()
        for c in kept_copies + c_copies:
            c.wait_send()

    @pl.when(gets_quarter)
    def _():
        z_copy.wait_send()
        for c in a_copies:
            c.wait_send()


def on_device(queries, keys, values, positions, tile_masks, sink_index):
    anywhere = pl.BlockSpec(memory_space=pl.ANY)
    dma = pltpu.SemaphoreType.DMA
    shard = (ROWS, HG * HD)
    return pl.pallas_call(
        kernel,
        out_shape=jax.ShapeDtypeStruct(shard, BF),
        in_specs=[anywhere] * 6,
        out_specs=pl.BlockSpec(memory_space=pltpu.VMEM),
        scratch_shapes=[
            pltpu.VMEM(shard, BF),
            pltpu.VMEM(shard, BF),
            pltpu.VMEM(shard, BF),
            pltpu.VMEM((3, ROWS), jnp.int32),
            pltpu.VMEM((1, SINK), jnp.int32),
            pltpu.SMEM((2, 2, 8), jnp.int32),
            pltpu.VMEM((5, HG, 2 * ROWS, HD), BF),
            pltpu.VMEM((2, HG, ROWS, HD), BF),
            pltpu.VMEM((8, ROWS), F32),
            pltpu.VMEM((8, ROWS), F32),
            pltpu.VMEM((8, ROWS), F32),
            pltpu.VMEM((2, HG, HD, ROWS), F32),
            pltpu.VMEM((2, HG, 8, ROWS), F32),
            pltpu.VMEM((HG, HD, ROWS), BF),
            pltpu.VMEM((HG, HD, ROWS), BF),
            pltpu.VMEM((HG, 8, ROWS), F32),
            pltpu.VMEM((2, SINK, HG * HD), BF),
            pltpu.VMEM((2, SINK, HG * HD), BF),
            pltpu.VMEM((SINK // 2, HG * HD), BF),
            pltpu.VMEM((len(KEPT), NY, CH, HG * HD), BF),
            pltpu.VMEM((len(KEPT), CH, HG * HD), BF),
            pltpu.VMEM((len(KEPT), CH, HG * HD), BF),
            pltpu.VMEM((len(KEPT), CH, HG * HD), BF),
            dma((6,)),
            dma((4, HG)), dma((4, HG)), dma((HG,)), dma((HG,)), dma, dma,
            dma((NX,)), dma, dma((len(KEPT), NY)), dma((len(KEPT), NY)), dma, dma,
            dma((len(KEPT),)), dma, dma((NY,)), dma((NY,)),
            dma((NX,)), dma((NX,)), dma((HG,)), dma((HG,)), dma((HG,)), dma((HG,)),
        ],
        compiler_params=pltpu.CompilerParams(
            collective_id=0, has_side_effects=True, vmem_limit_bytes=60 << 20
        ),
        cost_estimate=pl.CostEstimate(
            flops=2 * 10 * 2 * ROWS * ROWS * HD * HG, bytes_accessed=4 << 20,
            transcendentals=10 * ROWS * ROWS * HG,
        ),
    )(queries, keys, values, positions, sink_index[None, :], tile_masks.transpose(0, 2, 1))


def solution(mesh):
    in_specs = (
        P("tm", "heads"), P("tm", "heads"), P("tm", "heads"), P(None, "tm"), P("tm", None, None), P(),
    )
    return jax.shard_map(
        on_device, mesh=mesh, in_specs=in_specs, out_specs=P("tm", "heads"), check_vma=False
    )
```

time: 69 us -> 50.4 us (0.73)
  the two profiles are of different devices: /device:TPU:4 before, /device:TPU:20 now
where the time goes in v2:
time: 50.4 us; the launch traced here: 50.2 us
  Pallas kernels  48.6 us (96%)
  local copies, waits for them, and re-layouts  1.62 us (3%)
    pallas_call x1, Pallas kernels, on_device(): pl.pallas_call(kernel, out_shape=jax.ShapeDtypeStruct(shard, BF), in_spec...  48.6 us
    unnamed x1, local copies, waits for them, and re-layouts  1.62 us

profile of v2, /device:TPU:20, one launch (start us, length us, event | category | flops | bytes accessed | tf_op | source)
XLA Modules:
  0.0 50.2 jit_solution(902383563551713438)
XLA Ops:
  0.0 48.6 %shard_map.64 = bf16[256,384]{1,0:T(8,128)(2,1)} custom-call(bf16[256,384]{1,0:T(8,128)(2,1)} %q_hbm.1, bf16[256,384]{1,0:T(8,128)(2,1)} %k_hbm.1, bf16[256,384]{1,0:T(8,128)(2,1)} %v_hbm.1, s32[3,256]{1,0:T(4,128)} %pos_hbm.1, s32[1,256]{1,0:T(1,128)} %bitcast.3, s32[2,2,8]{2,1,0:T(2,128)} %bitcast.2), custom_call_target="tpu_custom_call" | custom-call | flops 1006632960 | bytes 4194304 | tf_op jit(solution)/shard_map/pallas_call | solution.py:474
  48.6 1.6 %copy.8 = bf16[256,384]{1,0:T(8,128)(2,1)} copy(bf16[256,384]{1,0:T(8,128)(2,1)} %shard_map.64) | data formatting | bytes 393216

commit v3 on v2

--- a/solution.py
+++ b/solution.py
@@ -159,6 +159,21 @@
     def send_kv(h):
         up[h].start()
         down[h].start()
+
+    def row_of(u, yy):
+        return pl.ds(pl.multiple_of((u // 2) * (SINK // 2) + yy * CH, CH), CH)
+
+    kept_copies = [
+        remote(
+            ptab.at[u % 2, row_of(u, (y + i) % NY)], scat.at[j, i], s_a.at[j, i], r_a.at[j, i], on_y(i)
+        )
+        for j, u in enumerate(KEPT) for i in range(1, NY)
+    ]
+
+    @pl.when(x == 0)
+    def _():
+        for c in kept_copies:
+            c.start()
 
     send_kv(0)
 
@@ -303,15 +318,6 @@
     def part_of(yy):
         return pl.ds(pl.multiple_of(yy * CH, CH), CH)
 
-    def row_of(u, yy):
-        return pl.ds(pl.multiple_of((u // 2) * (SINK // 2) + yy * CH, CH), CH)
-
-    kept_copies = [
-        remote(
-            ptab.at[u % 2, row_of(u, (y + i) % NY)], scat.at[j, i], s_a.at[j, i], r_a.at[j, i], on_y(i)
-        )
-        for j, u in enumerate(KEPT) for i in range(1, NY)
-    ]
     a_copies = [
         remote(quart.at[part_of((y + i) % NY)], scat.at[0, i], s_a.at[0, i], r_a.at[0, i], on_y(i))
         for i in range(1, NY)
@@ -339,11 +345,6 @@
     ]
 
     def sink_exchange():
-        @pl.when(x == 0)
-        def _():
-            for c in kept_copies:
-                c.start()
-
         @pl.when(gets_quarter)
         def _():
             spread(1).wait_recv()

time: 50.4 us -> 48.1 us (0.954)
  the two profiles are of different devices: /device:TPU:20 before, /device:TPU:8 now
where the time goes in v3:
time: 48.1 us; the launch traced here: 48 us
  Pallas kernels  46.3 us (96%)
  local copies, waits for them, and re-layouts  1.62 us (3%)
    pallas_call x1, Pallas kernels, on_device(): pl.pallas_call(kernel, out_shape=jax.ShapeDtypeStruct(shard, BF), in_spec...  46.3 us
    unnamed x1, local copies, waits for them, and re-layouts  1.62 us

profile of v3, /device:TPU:8, one launch (start us, length us, event | category | flops | bytes accessed | tf_op | source)
XLA Modules:
  0.0 48.0 jit_solution(17708810936264669687)
XLA Ops:
  0.0 46.3 %shard_map.64 = bf16[256,384]{1,0:T(8,128)(2,1)} custom-call(bf16[256,384]{1,0:T(8,128)(2,1)} %q_hbm.1, bf16[256,384]{1,0:T(8,128)(2,1)} %k_hbm.1, bf16[256,384]{1,0:T(8,128)(2,1)} %v_hbm.1, s32[3,256]{1,0:T(4,128)} %pos_hbm.1, s32[1,256]{1,0:T(1,128)} %bitcast.3, s32[2,2,8]{2,1,0:T(2,128)} %bitcast.2), custom_call_target="tpu_custom_call" | custom-call | flops 1006632960 | bytes 4194304 | tf_op jit(solution)/shard_map/pallas_call | solution.py:475
  46.4 1.6 %copy.8 = bf16[256,384]{1,0:T(8,128)(2,1)} copy(bf16[256,384]{1,0:T(8,128)(2,1)} %shard_map.64) | data formatting | bytes 393216

commit v4 on v3

--- a/solution.py
+++ b/solution.py
@@ -157,8 +157,18 @@
             spread(i).start()
 
     def send_kv(h):
-        up[h].start()
-        down[h].start()
+        @pl.when(p < NP - 1)
+        def _():
+            up[h].start()
+
+        @pl.when(p > 0)
+        def _():
+            down[h].start()
+
+    for slot, absent in ((0, p < 2), (1, p < 1), (3, p > NP - 2), (4, p > NP - 3)):
+        @pl.when(absent)
+        def _(slot=slot):
+            kv[slot] = jnp.zeros((HG, 2 * ROWS, HD), BF)
 
     def row_of(u, yy):
         return pl.ds(pl.multiple_of((u // 2) * (SINK // 2) + yy * CH, CH), CH)
@@ -273,10 +283,21 @@
         return (lambda: tab[0, :, cols], value, None)
 
     def hop(h):
-        up[h].wait_recv()
-        up2[h].start()
-        down[h].wait_recv()
-        down2[h].start()
+        @pl.when(p > 0)
+        def _():
+            up[h].wait_recv()
+
+        @pl.when((p > 0) & (p < NP - 1))
+        def _():
+            up2[h].start()
+
+        @pl.when(p < NP - 1)
+        def _():
+            down[h].wait_recv()
+
+        @pl.when((p > 0) & (p < NP - 1))
+        def _():
+            down2[h].start()
 
     def near_blocks(h):
         q_copies[h].wait_recv()
@@ -298,8 +319,14 @@
     ]
 
     def far_blocks(h):
-        up2[h].wait_recv()
-        down2[h].wait_recv()
+        @pl.when(p > 1)
+        def _():
+            up2[h].wait_recv()
+
+        @pl.when(p < NP - 2)
+        def _():
+            down2[h].wait_recv()
+
         attend(1, h, [shard_block(far, h, their_rows(3, 0))])
         o_send[h] = acc[1, h].astype(BF)
         o_copies[h].start()
@@ -450,7 +477,21 @@
         for i in spread_to:
             spread(i).wait_send()
 
-    for group in (q_copies, up, down, up2, down2, o_copies, ml_copies, y_copies, x_copies):
+    for h in range(HG):
+        @pl.when(p < NP - 1)
+        def _(h=h):
+            up[h].wait_send()
+
+        @pl.when(p > 0)
+        def _(h=h):
+            down[h].wait_send()
+
+        @pl.when((p > 0) & (p < NP - 1))
+        def _(h=h):
+            up2[h].wait_send()
+            down2[h].wait_send()
+
+    for group in (q_copies, o_copies, ml_copies, y_copies, x_copies):
         for c in group:
             c.wait_send()
     bias_copy.wait_send()
@@ -508,7 +549,7 @@
             dma((NX,)), dma((NX,)), dma((HG,)), dma((HG,)), dma((HG,)), dma((HG,)),
         ],
         compiler_params=pltpu.CompilerParams(
-            collective_id=0, has_side_effects=True, vmem_limit_bytes=60 << 20
+            collective_id=0, has_side_effects=True, vmem_limit_bytes=55000 << 10
         ),
         cost_estimate=pl.CostEstimate(
             flops=2 * 10 * 2 * ROWS * ROWS * HD * HG, bytes_accessed=4 << 20,

time: 48.1 us -> 47.6 us (0.990)
  the two profiles are of different devices: /device:TPU:8 before, /device:TPU:16 now
where the time goes in v4:
time: 47.6 us; the launch traced here: 47.4 us
  Pallas kernels  45.4 us (95%)
  local copies, waits for them, and re-layouts  2.06 us (4%)
    pallas_call x1, Pallas kernels, on_device(): pl.pallas_call(kernel, out_shape=jax.ShapeDtypeStruct(shard, BF), in_spec...  45.4 us
    unnamed x7, local copies, waits for them, and re-layouts  2.06 us

profile of v4, /device:TPU:16, one launch (start us, length us, event | category | flops | bytes accessed | tf_op | source)
XLA Modules:
  0.0 47.4 jit_solution(13854890078211216969)
XLA Ops:
  0.0 0.0 copy-start.1
  0.0 0.0 copy-start.2
  0.0 0.7 %copy-done.1 = s32[2,8,2]{1,2,0:T(2,128)S(1)} copy-done((s32[2,8,2]{1,2,0:T(2,128)S(1)}, s32[2,8,2]{1,2,0:T(2,128)}, u32[]{:S(2)}) %copy-start.1) | copy-done | bytes 152
  0.7 0.0 copy-done.2
  0.7 0.0 copy-start
  0.7 0.7 %copy-done = s32[3,256]{1,0:T(4,128)S(1)} copy-done((s32[3,256]{1,0:T(4,128)S(1)}, s32[3,256]{1,0:T(4,128)}, u32[]{:S(2)}) %copy-start) | copy-done | bytes 3096
  1.4 45.4 %shard_map.64 = bf16[256,384]{1,0:T(8,128)(2,1)S(1)} custom-call(bf16[256,384]{1,0:T(8,128)(2,1)} %q_hbm.1, bf16[256,384]{1,0:T(8,128)(2,1)} %k_hbm.1, bf16[256,384]{1,0:T(8,128)(2,1)} %v_hbm.1, s32[3,256]{1,0:T(4,128)S(1)} %copy-done, s32[1,256]{1,0:T(1,128)S(1)} %bitcast.3, s32[2,2,8]{2,1,0:T(2,128)S(1)} %bitcast.2), custom_call_target="tpu_custom_call" | custom-call | flops 1006632960 | bytes 4194304 | tf_op jit(solution)/shard_map/pallas_call | solution.py:516
  46.8 0.7 %copy.8 = bf16[256,384]{1,0:T(8,128)(2,1)} copy(bf16[256,384]{1,0:T(8,128)(2,1)S(1)} %shard_map.64) | data formatting | bytes 393216
Async XLA Ops:
  0.0 0.7 %copy-start.1 = (s32[2,8,2]{1,2,0:T(2,128)S(1)}, s32[2,8,2]{1,2,0:T(2,128)}, u32[]{:S(2)}) copy-start(s32[2,8,2]{1,2,0:T(2,128)} %param.10) | copy-start | bytes 388
  0.0 0.7 %copy-start.2 = (s32[256]{0:T(256)S(1)}, s32[256]{0:T(256)}, u32[]{:S(2)}) copy-start(s32[256]{0:T(256)} %param.11) | copy-start | bytes 3076
  0.7 0.7 %copy-start = (s32[3,256]{1,0:T(4,128)S(1)}, s32[3,256]{1,0:T(4,128)}, u32[]{:S(2)}) copy-start(s32[3,256]{1,0:T(4,128)} %pos_hbm.1) | copy-start | bytes 9220

commit v5 on v4

--- a/solution.py
+++ b/solution.py
@@ -432,9 +432,9 @@
 
     attend(0, 0, [shard_block(2, 0, None)])
     send_kv(1)
+    sink_exchange()
     attend(0, 1, [shard_block(2, 1, None)])
     attend(0, 2, [shard_block(2, 2, None)])
-    sink_exchange()
     hop(0)
     send_kv(2)
     bias_copy.wait_recv()

time: 47.6 us -> 47.6 us (level)
  no operation moved by 1% of the time
where the time goes in v5:
time: 47.6 us; the launch traced here: 47.4 us
  Pallas kernels  45.4 us (95%)
  local copies, waits for them, and re-layouts  2.06 us (4%)
    pallas_call x1, Pallas kernels, on_device(): pl.pallas_call(kernel, out_shape=jax.ShapeDtypeStruct(shard, BF), in_spec...  45.4 us
    unnamed x7, local copies, waits for them, and re-layouts  2.06 us

profile of v5, /device:TPU:16, one launch (start us, length us, event | category | flops | bytes accessed | tf_op | source)
XLA Modules:
  0.0 47.4 jit_solution(16363162118436252300)
XLA Ops:
  0.0 0.0 copy-start.1
  0.0 0.0 copy-start.2
  0.0 0.7 %copy-done.1 = s32[2,8,2]{1,2,0:T(2,128)S(1)} copy-done((s32[2,8,2]{1,2,0:T(2,128)S(1)}, s32[2,8,2]{1,2,0:T(2,128)}, u32[]{:S(2)}) %copy-start.1) | copy-done | bytes 152
  0.7 0.0 copy-done.2
  0.7 0.0 copy-start
  0.7 0.7 %copy-done = s32[3,256]{1,0:T(4,128)S(1)} copy-done((s32[3,256]{1,0:T(4,128)S(1)}, s32[3,256]{1,0:T(4,128)}, u32[]{:S(2)}) %copy-start) | copy-done | bytes 3096
  1.4 45.4 %shard_map.64 = bf16[256,384]{1,0:T(8,128)(2,1)S(1)} custom-call(bf16[256,384]{1,0:T(8,128)(2,1)} %q_hbm.1, bf16[256,384]{1,0:T(8,128)(2,1)} %k_hbm.1, bf16[256,384]{1,0:T(8,128)(2,1)} %v_hbm.1, s32[3,256]{1,0:T(4,128)S(1)} %copy-done, s32[1,256]{1,0:T(1,128)S(1)} %bitcast.3, s32[2,2,8]{2,1,0:T(2,128)S(1)} %bitcast.2), custom_call_target="tpu_custom_call" | custom-call | flops 1006632960 | bytes 4194304 | tf_op jit(solution)/shard_map/pallas_call | solution.py:516
  46.8 0.7 %copy.8 = bf16[256,384]{1,0:T(8,128)(2,1)} copy(bf16[256,384]{1,0:T(8,128)(2,1)S(1)} %shard_map.64) | data formatting | bytes 393216
Async XLA Ops:
  0.0 0.7 %copy-start.1 = (s32[2,8,2]{1,2,0:T(2,128)S(1)}, s32[2,8,2]{1,2,0:T(2,128)}, u32[]{:S(2)}) copy-start(s32[2,8,2]{1,2,0:T(2,128)} %param.10) | copy-start | bytes 388
  0.0 0.7 %copy-start.2 = (s32[256]{0:T(256)S(1)}, s32[256]{0:T(256)}, u32[]{:S(2)}) copy-start(s32[256]{0:T(256)} %param.11) | copy-start | bytes 3076
  0.7 0.7 %copy-start = (s32[3,256]{1,0:T(4,128)S(1)}, s32[3,256]{1,0:T(4,128)}, u32[]{:S(2)}) copy-start(s32[3,256]{1,0:T(4,128)} %pos_hbm.1) | copy-start | bytes 9220
